TPU v7x, 512 devices: a whole 4x8x8 slice. The times are simulated.
512 devices in a mesh: wide: 64 (over y_hi, z, core), tp: 8 (over x, y_lo).
Axes of the slice: x: 4, y: 8 (y_hi: 4, y_lo: 2; y = y_hi * 2 + y_lo), z: 8, core: 2. Of those that a mesh axis runs over, the one named last changes fastest.
Arguments:
- queries: bfloat16 [64, 128, 128], P('wide', 'tp'), may hold values from -384 to 384, as said below
- new_keys: bfloat16 [64, 8, 128], P('wide', 'tp'), may hold values from -9 to 9
- new_values: bfloat16 [64, 8, 128], P('wide', 'tp'), may hold values from -6 to 6
- prefix_keys: bfloat16 [256, 128, 8, 128], P('wide', None, 'tp'), may hold values from -6 to 6
- prefix_values: bfloat16 [256, 128, 8, 128], P('wide', None, 'tp'), may hold values from -6 to 6
- suffix_keys: bfloat16 [64, 512, 8, 128], P('wide', None, 'tp'), may hold values from -6 to 6
- suffix_values: bfloat16 [64, 512, 8, 128], P('wide', None, 'tp'), may hold values from -6 to 6
- lengths: int32 [64], P('wide'), may hold values from 1 to 512, as said below
- page_table: int32 [128], replicated, may hold values from 0 to 255, as said below
- out_weight: bfloat16 [16384, 16384], P('tp', 'wide'), may hold values from -3.59375 to 3.59375
Outputs:
- mixed: float32 [64, 16384], P('tp', 'wide')
Inputs may be any that keep to these rules, and one draw needn't show every extreme that they name: `queries`: at most 384 in magnitude. `lengths`: some request has exactly 512 live slots. `page_table`: distinct pages; page 0 and page 256 - 1 are always among them.
All inputs are finite; a program needn't handle non-finite values.
Results may differ from a plain program's by a relative error of at most 0.013.
Values may be sent and summed in bfloat16 or wider, within the bound.
A program may use at most 128 MiB of HBM per device.

v0:
```python
import math

import jax
import jax.numpy as jnp
from jax import lax
from jax.sharding import PartitionSpec as P


def joined_2(part, axis, combine):
    gathered = jax.tree.map(lambda a: lax.all_gather(a, axis), part)

    def take(source):
        return jax.tree.map(lambda a: lax.dynamic_index_in_dim(a, source, 0, False), gathered)

    return lax.fori_loop(
        1, lax.axis_size(axis), lambda source, state: combine(state, take(source)), take(0)
    )


def combine_partials(earlier, later_part):
    max_one, mass_one, acc_one = earlier
    max_two, mass_two, acc_two = later_part
    joined = jnp.maximum(max_one, max_two)
    factor_one = jnp.exp(max_one - joined)
    factor_two = jnp.exp(max_two - joined)
    return (
        joined,
        mass_one * factor_one + mass_two * factor_two,
        acc_one * factor_one[..., None] + acc_two * factor_two[..., None],
    )


def local(
    queries,
    new_keys,
    new_values,
    prefix_keys,
    prefix_values,
    suffix_keys,
    suffix_values,
    lengths,
    page_table,
    out_weight,
):
    req_dev, heads_dev, head_dim = queries.shape
    kv_dev = new_keys.shape[1]
    group_size = heads_dev // kv_dev
    my_index = lax.axis_index("wide")
    score_scale = head_dim ** (-0.5)
    pool_dev, page_len = (prefix_keys.shape[0], prefix_keys.shape[1])
    suf_len = suffix_keys.shape[1]
    all_queries = lax.all_gather(queries, "wide", axis=0, tiled=True)
    total_req = all_queries.shape[0]
    page_ids = my_index * pool_dev + jnp.arange(pool_dev, dtype=jnp.int32)
    used_pages = jnp.any(page_table[None, :] == page_ids[:, None], axis=1)
    keep_mask = jnp.repeat(used_pages, page_len)
    pool_keys = prefix_keys.reshape(pool_dev * page_len, kv_dev, head_dim)
    pool_values = prefix_values.reshape(pool_dev * page_len, kv_dev, head_dim)
    row_block = math.gcd(total_req, 64)
    grouped = all_queries.reshape(total_req // row_block, row_block, kv_dev, group_size, head_dim)

    def prefix_block(query_block):
        scores = (
            jnp.einsum("nghd,kgd->nghk", query_block, pool_keys, preferred_element_type=jnp.float32)
            * score_scale
        )
        scores = jnp.where(keep_mask, scores, -1e30)
        maxima = jnp.max(scores, axis=-1)
        weights = jnp.where(keep_mask, jnp.exp(scores - maxima[..., None]), 0.0)
        masses = jnp.sum(weights, axis=-1)
        accums = jnp.einsum(
            "nghk,kgd->nghd",
            weights.astype(jnp.bfloat16),
            pool_values,
            preferred_element_type=jnp.float32,
        )
        return (maxima, masses, accums)

    maxima, masses, accums = lax.map(prefix_block, grouped)
    maxima = maxima.reshape(total_req, kv_dev, group_size)
    masses = masses.reshape(total_req, kv_dev, group_size)
    accums = accums.reshape(total_req, kv_dev, group_size, head_dim)
    own_start = my_index * req_dev
    whole = joined_2((maxima, masses, accums), "wide", combine_partials)
    own_max = lax.dynamic_slice_in_dim(whole[0], own_start, req_dev, 0)
    own_mass = lax.dynamic_slice_in_dim(whole[1], own_start, req_dev, 0)
    own_acc = lax.dynamic_slice_in_dim(whole[2], own_start, req_dev, 0)
    own_queries = queries.reshape(req_dev, kv_dev, group_size, head_dim)
    suf_scores = (
        jnp.einsum("rghd,rsgd->rghs", own_queries, suffix_keys, preferred_element_type=jnp.float32)
        * score_scale
    )
    live_mask = (jnp.arange(suf_len, dtype=jnp.int32)[None, :] < lengths[:, None])[:, None, None, :]
    suf_scores = jnp.where(live_mask, suf_scores, -1e30)
    own_score = (
        jnp.einsum("rghd,rgd->rgh", own_queries, new_keys, preferred_element_type=jnp.float32)
        * score_scale
    )
    row_max = jnp.maximum(jnp.maximum(own_max, jnp.max(suf_scores, axis=-1)), own_score)
    suf_weights = jnp.where(live_mask, jnp.exp(suf_scores - row_max[..., None]), 0.0)
    own_weight = jnp.exp(own_score - row_max)
    rescale = jnp.exp(own_max - row_max)
    total = own_mass * rescale + jnp.sum(suf_weights, axis=-1) + own_weight
    summed = own_acc * rescale[..., None]
    summed = summed + jnp.einsum(
        "rghs,rsgd->rghd",
        suf_weights.astype(jnp.bfloat16),
        suffix_values,
        preferred_element_type=jnp.float32,
    )
    own_round = lax.optimization_barrier(own_weight.astype(jnp.bfloat16)).astype(jnp.float32)
    summed = summed + own_round[..., None] * new_values.astype(jnp.float32)[:, :, None, :]
    attn = (summed / total[..., None]).astype(jnp.bfloat16).reshape(req_dev, heads_dev * head_dim)
    terms = jnp.dot(
        lax.all_gather(attn, "wide", axis=0, tiled=True),
        out_weight,
        preferred_element_type=jnp.float32,
    )
    return lax.psum_scatter(terms, "tp", scatter_dimension=0, tiled=True)


def solution(mesh):
    in_specs = (
        P("wide", "tp", None),
        P("wide", "tp", None),
        P("wide", "tp", None),
        P("wide", None, "tp", None),
        P("wide", None, "tp", None),
        P("wide", None, "tp", None),
        P("wide", None, "tp", None),
        P("wide"),
        P(),
        P("tp", "wide"),
    )
    out_specs = P("tp", "wide")
    return jax.shard_map(local, mesh=mesh, in_specs=in_specs, out_specs=out_specs, check_vma=False)
```

profile of v0, /device:TPU:1, one launch (start us, length us, event | category | flops | bytes accessed | tf_op | source)
XLA Modules:
  0.0 545.4 jit_solution(13755772067987513848)
XLA Ops:
  7.5 91.1 %all_gather.15 = bf16[64,16,128]{2,1,0:T(8,128)(2,1)S(1)} all-gather(bf16[1,16,128]{2,1,0:T(8,128)(2,1)} %param.12), channel_id=1, replica_groups=mesh['wide'=64,'tp'=8] {'wide'}, dimensions={0}, use_global_device_ids=true | all-gather | bytes 266240 | tf_op jit(solution)/shard_map/all_gather | solution.py:52
  101.0 1.5 convolution_bitcast_fusion
  103.4 83.0 %all-gather.4 = f32[64,64,16]{1,2,0:T(8,128)S(1)} all-gather(f32[1,64,16]{1,2,0:T(8,128)S(1)} %bitcast.162), channel_id=3, replica_groups=mesh['wide'=64,'tp'=8] {'wide'}, dimensions={0}, use_global_device_ids=true | all-gather | bytes 266240 | tf_op jit(solution)/shard_map/all_gather | solution.py:10
  186.4 86.5 %all-gather.3 = f32[64,64,16]{1,2,0:T(8,128)S(1)} all-gather(f32[1,64,16]{1,2,0:T(8,128)S(1)} %bitcast.161), channel_id=2, replica_groups=mesh['wide'=64,'tp'=8] {'wide'}, dimensions={0}, use_global_device_ids=true | all-gather | bytes 266240 | tf_op jit(solution)/shard_map/all_gather | solution.py:10
  273.1 40.0 %all-gather.8.cloned.1.call-done = f32[4096,1,16,128]{3,2,1,0:T(8,128)} async-done(((f32[64,1,16,128]{3,2,1,0:T(8,128)}), f32[4096,1,16,128]{3,2,1,0:T(8,128)}) %all-gather.8.cloned.1.call-update) | async-done | bytes 33554448 | tf_op jit(solution)/shard_map/all_gather | solution.py:10
  314.2 106.0 %while.12 = (s32[]{:T(128)}, f32[64,1,16]{0,2,1:T(8,128)S(1)}, f32[64,1,16]{0,2,1:T(8,128)S(1)}, f32[64,1,16,128]{3,2,1,0:T(8,128)S(1)}, f32[64,64,1,16]{1,3,2,0...) while((s32[]{:T(128)}, f32[64,1,16]{0,2,1:T(8,128)S(1)}, ...), condition=%wide.region_4.5_spmd, body=%wide.region_3.4_spmd.sunk | while | flops 400389 | bytes 1650843 | solution.py:15
  314.4 1.4 fusion.52
  316.1 1.4 fusion.52
  317.8 1.4 fusion.52
  319.5 1.4 fusion.52
  324.5 1.4 fusion.52
  326.2 1.4 fusion.52
  327.9 1.4 fusion.52
  329.6 1.4 fusion.52
  331.3 1.4 fusion.52
  333.0 1.4 fusion.52
  334.6 1.4 fusion.52
  339.7 1.4 fusion.52
  341.4 1.4 fusion.52
  343.1 1.4 fusion.52
  344.7 1.4 fusion.52
  346.4 1.4 fusion.52
  348.1 1.4 fusion.52
  349.8 1.4 fusion.52
  351.5 1.4 fusion.52
  356.5 1.4 fusion.52
  358.2 1.4 fusion.52
  359.9 1.4 fusion.52
  361.6 1.4 fusion.52
  363.3 1.4 fusion.52
  364.9 1.4 fusion.52
  366.6 1.4 fusion.52
  371.7 1.4 fusion.52
  373.4 1.4 fusion.52
  375.0 1.4 fusion.52
  376.7 1.4 fusion.52
  378.4 1.4 fusion.52
  380.1 1.4 fusion.52
  381.8 1.4 fusion.52
  383.5 1.4 fusion.52
  388.5 1.4 fusion.52
  390.2 1.4 fusion.52
  391.9 1.4 fusion.52
  393.6 1.4 fusion.52
  395.2 1.4 fusion.52
  396.9 1.4 fusion.52
  420.9 82.6 %all-gather.5 = bf16[64,1,2048]{2,1,0:T(2,128)(2,1)S(1)} all-gather(bf16[1,1,2048]{2,1,0:T(2,128)(2,1)S(1)} %reshape.207), channel_id=1, replica_groups=mesh['wide'=64,'tp'=8] {'wide'}, dimensions={0}, use_global_device_ids=true | all-gather | bytes 266240 | tf_op jit(solution)/shard_map/all_gather | solution.py:115
  504.4 34.1 %reduce-scatter.2.cloned.1.call-done = f32[8,256]{1,0:T(8,128)} async-done(((f32[64,256]{1,0:T(8,128)}), f32[8,256]{1,0:T(8,128)}) %reduce-scatter.2.cloned.1.call-update) | async-done | bytes 8208 | tf_op jit(solution)/shard_map/reduce_scatter | solution.py:119
  (377 shorter events, 52.1 us)
Async XLA Ops:
  6.5 496.9 %copy-start = (bf16[2048,256]{1,0:T(8,128)(2,1)S(1)}, bf16[2048,256]{1,0:T(8,128)(2,1)}, u32[]{:S(2)}) copy-start(bf16[2048,256]{1,0:T(8,128)(2,1)} %param.21) | copy-start | bytes 3145732
  6.5 306.6 %all-gather.8.cloned.1.call-start = ((), (), s32[]{:S(2)}) async-start(), calls=%async_computation.2 | async-start | bytes 34078720 | tf_op jit(solution)/shard_map/all_gather | solution.py:10
  100.0 0.9 copy-start.2
  100.1 3.2 copy-start.3
  100.1 3.2 copy-start.5
  100.8 172.1 %copy-start.6 = (bf16[1,1,128]{2,1,0:T(2,128)(2,1)S(1)}, bf16[1,1,128]{2,1,0:T(2,128)(2,1)}, u32[]{:S(2)}) copy-start(bf16[1,1,128]{2,1,0:T(2,128)(2,1)} %param.14) | copy-start | bytes 772
  100.8 172.1 %copy-start.1 = (bf16[1,512,1,128]{3,1,2,0:T(8,128)(2,1)S(1)}, bf16[1,512,1,128]{3,1,2,0:T(8,128)(2,1)}, u32[]{:S(2)}) copy-start(bf16[1,512,1,128]{3,1,2,0:T(8,128)(2,1)} %param.17) | copy-start | bytes 393220
  102.5 436.0 %reduce-scatter.2.cloned.1.call-start = ((), (), s32[]{:S(2)}) async-start(), calls=%async_computation.1 | async-start | bytes 73728 | tf_op jit(solution)/shard_map/reduce_scatter | solution.py:119
  314.2 106.5 %copy-start.4 = (bf16[1,512,1,128]{3,1,2,0:T(8,128)(2,1)S(1)}, bf16[1,512,1,128]{3,1,2,0:T(8,128)(2,1)}, u32[]{:S(2)}) copy-start(bf16[1,512,1,128]{3,1,2,0:T(8,128)(2,1)} %param.18) | copy-start | bytes 393220
Sparse Core Ops, SparseCore 0:
  102.6 210.4 all-gather.7
  504.6 33.9 reduce-scatter.1
where the time goes:
time: 553 us; the launch traced here: 545 us
  blocking collectives  343 us (62%)
  other arithmetic  94.4 us (17%)
  waiting for transfers between devices  74.1 us (13%)
  between operations  14.2 us (3%)
  local copies, waits for them, and re-layouts  12.1 us (2%)
    all_gather x2, blocking collectives, joined_2(): gathered = jax.tree.map(lambda a: lax.all_gather(a, axis), part)  170 us
    all_gather x1, blocking collectives, local(): all_queries = lax.all_gather(queries, 'wide', axis=0, tiled=True)  91.1 us
    add x63, other arithmetic, combine_partials(): acc_one * factor_one[..., None] + acc_two * factor_two[..., None]  90.5 us
    all_gather x1, blocking collectives, local(): lax.all_gather(attn, 'wide', axis=0, tiled=True)  82.6 us
    all_gather x1, waiting for transfers between devices, joined_2(): gathered = jax.tree.map(lambda a: lax.all_gather(a, axis), part)  40 us
    reduce_scatter x1, waiting for transfers between devices, local(): return lax.psum_scatter(terms, 'tp', scatter_dimension=0, tiled=True)  34.1 us
  transfers between devices with their start and end apart: 2, of which 2 were waited for; matrix products, arithmetic and copies ran while one was open for 0% of the time, Pallas kernels for 0%

commit v1 on v0

v1 whole, which is shorter than its diff:
```python
import functools

import jax
import jax.numpy as jnp
from jax import lax
from jax.experimental import pallas as pl
from jax.experimental.pallas import tpu as pltpu
from jax.sharding import PartitionSpec as P

MESH = pl.DeviceIdType.MESH
NY, NZ = 4, 8
NX, NL = 4, 2
CHIPS = NY * NZ
WIDE = [(a, b) for a in (2, 1, 3, 0) for b in (4, 3, 5, 2, 6, 1, 7, 0) if (a, b) != (0, 0)]
TP = [(a, b, d) for a in (2, 1, 3, 0) for b in (1, 0) for d in (1, 0) if (a, b, d) != (0, 0, 0)]
LOG2E = 1.4426950408889634


def kernel(
    len_ref,
    q_hbm,
    nk_hbm,
    nv_hbm,
    pk_hbm,
    pv_hbm,
    sk_hbm,
    sv_hbm,
    pt_hbm,
    w_hbm,
    o_ref,
    qbuf,
    kbuf,
    vbuf,
    ktbuf,
    skbuf,
    svbuf,
    nkbuf,
    nvbuf,
    ptbuf,
    wbuf,
    acc_out,
    st_out,
    acc_in,
    st_in,
    attn_buf,
    attn32,
    proj_out,
    proj_in,
    local_sem,
    q_send,
    q_recv,
    core_send,
    core_recv,
    acc_send,
    acc_recv,
    st_send,
    st_recv,
    attn_send,
    attn_recv,
    proj_send,
    proj_recv,
):
    heads, hd = q_hbm.shape
    tokens = pk_hbm.shape[0]
    rows = NZ * heads
    scale = hd ** (-0.5) * LOG2E
    wide = lax.axis_index("wide")
    tp = lax.axis_index("tp")
    y, z, c = wide // (2 * NZ), (wide // 2) % NZ, wide % 2
    x, low = tp // NL, tp % NL

    def wide_at(a, b, sign=1):
        return (((y + sign * a + NY) % NY) * (2 * NZ) + ((z + sign * b + NZ) % NZ) * 2 + c, tp)

    def tp_at(a, b, d):
        return (wide - c + (c + d) % 2, ((x + a) % NX) * NL + (low + b) % NL)

    partner = tp_at(0, 0, 1)

    barrier = pltpu.get_barrier_semaphore()
    for a, b in WIDE:
        pl.semaphore_signal(barrier, inc=1, device_id=wide_at(a, b), device_id_type=MESH)
    for a, b, d in TP:
        pl.semaphore_signal(barrier, inc=1, device_id=tp_at(a, b, d), device_id_type=MESH)

    loads = [
        (q_hbm, qbuf.at[0, pl.ds(0, heads)]),
        (sk_hbm, skbuf),
        (sv_hbm, svbuf),
        (nk_hbm, nkbuf),
        (nv_hbm, nvbuf),
        (pt_hbm, ptbuf),
        (pk_hbm, kbuf.at[0]),
        (pv_hbm, vbuf.at[0]),
        (w_hbm, wbuf.at[0]),
    ]
    loads = [pltpu.make_async_copy(src, dst, local_sem.at[i]) for i, (src, dst) in enumerate(loads)]
    for load in loads:
        load.start()
    for load in loads[:6]:
        load.wait()

    own_q = qbuf[0, :heads]
    length = len_ref[0]
    slots = skbuf.shape[0]
    scores = lax.dot_general(
        own_q, skbuf[...], (((1,), (1,)), ((), ())), preferred_element_type=jnp.float32
    )
    live = lax.broadcasted_iota(jnp.int32, (heads, slots), 1) < length
    scores = jnp.where(live, scores, -1e30)
    new_score = jnp.sum(
        own_q.astype(jnp.float32) * nkbuf[...].astype(jnp.float32), axis=1, keepdims=True
    )
    suf_max = jnp.maximum(jnp.max(scores, axis=1, keepdims=True), new_score)
    weights = jnp.exp2((scores - suf_max) * scale)
    new_weight = jnp.exp2((new_score - suf_max) * scale)
    suf_mass = jnp.sum(weights, axis=1, keepdims=True) + new_weight
    suf_acc = jnp.dot(weights.astype(jnp.bfloat16), svbuf[...], preferred_element_type=jnp.float32)
    suf_acc = suf_acc + new_weight.astype(jnp.bfloat16).astype(jnp.float32) * nvbuf[...].astype(
        jnp.float32
    )
    suf_max = suf_max * scale

    pages = tokens // 128
    bias = []
    for half in range(2):
        first = (wide - c + (c + half) % 2) * pages
        for page in range(pages):
            used = jnp.max((ptbuf[...] == first + page).astype(jnp.float32), axis=1, keepdims=True)
            bias.append(jnp.broadcast_to((used - 1.0) * 1e30, (1, 128)))
    bias = jnp.concatenate(bias, axis=1)

    for load in loads[6:]:
        load.wait()
    ktbuf[:, :tokens] = kbuf[0].T

    pl.semaphore_wait(barrier, len(WIDE) + len(TP))

    for a, b in WIDE:
        pltpu.make_async_remote_copy(
            qbuf.at[0, pl.ds(0, heads)],
            qbuf.at[a, pl.ds(b * heads, heads)],
            q_send,
            q_recv.at[a],
            device_id=wide_at(a, b),
            device_id_type=MESH,
        ).start()
    swaps = [
        pltpu.make_async_remote_copy(
            buf.at[0],
            buf.at[1],
            core_send.at[i],
            core_recv.at[i],
            device_id=partner,
            device_id_type=MESH,
        )
        for i, buf in enumerate((kbuf, vbuf, wbuf))
    ]
    for swap in swaps:
        swap.start()
    swaps[0].wait_recv()
    ktbuf[:, tokens:] = kbuf[1].T
    swaps[1].wait_recv()
    values = vbuf[...].reshape(2 * tokens, hd)

    def landed(ref, sem):
        pltpu.make_async_copy(ref, ref, sem).wait()

    lane = lax.broadcasted_iota(jnp.int32, (rows, 128), 1)
    for a in (0, 1, 3, 2):
        landed(qbuf.at[0, pl.ds(heads, rows - heads)] if a == 0 else qbuf.at[a], q_recv.at[a])
        s = jnp.dot(qbuf[a], ktbuf[...], preferred_element_type=jnp.float32) + bias
        top = jnp.max(s, axis=1, keepdims=True)
        p = jnp.exp2((s - top) * scale)
        mass = jnp.sum(p, axis=1, keepdims=True)
        acc = jnp.dot(p.astype(jnp.bfloat16), values, preferred_element_type=jnp.float32)
        acc_out[a] = acc.astype(jnp.bfloat16)
        stats = jnp.where(lane == 0, top * scale, jnp.where(lane == 1, mass, 0.0))
        st_out[a] = stats.T[:2]
        for b in (4, 3, 5, 2, 6, 1, 7, 0):
            if (a, b) == (0, 0):
                continue
            pltpu.make_async_remote_copy(
                st_out.at[a],
                st_in.at[a, b],
                st_send,
                st_recv.at[a],
                device_id=wide_at(a, b, -1),
                device_id_type=MESH,
            ).start()
            pltpu.make_async_remote_copy(
                acc_out.at[a, pl.ds(b * heads, heads)],
                acc_in.at[a, pl.ds(b * heads, heads)],
                acc_send,
                acc_recv.at[a],
                device_id=wide_at(a, b, -1),
                device_id_type=MESH,
            ).start()
        if a == 0:
            acc_in[0, :heads] = acc_out[0, :heads]
            st_in[0, 0] = st_out[0]

    spot = lax.broadcasted_iota(jnp.int32, (2, rows), 1) // heads
    joined = []
    for a in range(NY):
        landed(st_in.at[0, pl.ds(1, NZ - 1)] if a == 0 else st_in.at[a], st_recv.at[a])
        line = jnp.zeros((2, rows), jnp.float32)
        for b in range(NZ):
            line = jnp.where(spot == b, st_in[a, b], line)
        joined.append(line)
    tops = jnp.concatenate([line[:1] for line in joined], axis=0)
    masses = jnp.concatenate([line[1:] for line in joined], axis=0)
    best = jnp.broadcast_to(jnp.max(tops, axis=0, keepdims=True), (8, rows))
    for shift in (heads, 2 * heads, 4 * heads):
        best = jnp.maximum(best, pltpu.roll(best, shift, 1))
    factors = jnp.exp2(tops - best[:1])
    mass_line = jnp.sum(factors * masses, axis=0, keepdims=True)
    mine = lax.broadcasted_iota(jnp.int32, (heads, rows), 1) % heads == lax.broadcasted_iota(
        jnp.int32, (heads, rows), 0
    )
    pre_max = jnp.max(jnp.where(mine, best[:1], -3e38), axis=1, keepdims=True)
    pre_mass = jnp.sum(jnp.where(mine, mass_line, 0.0), axis=1, keepdims=True)
    pre_acc = jnp.zeros((2 * heads, hd), jnp.float32)
    for a in range(NY):
        spread = jnp.where(mine, factors[a : a + 1], 0.0)
        high = spread.astype(jnp.bfloat16)
        rest = (spread - high.astype(jnp.float32)).astype(jnp.bfloat16)
        landed(acc_in.at[0, pl.ds(heads, rows - heads)] if a == 0 else acc_in.at[a], acc_recv.at[a])
        pre_acc = pre_acc + jnp.dot(
            jnp.concatenate([high, rest], axis=0), acc_in[a], preferred_element_type=jnp.float32
        )
    row_max = jnp.maximum(pre_max, suf_max)
    pre_factor = jnp.exp2(pre_max - row_max)
    suf_factor = jnp.exp2(suf_max - row_max)
    total = pre_mass * pre_factor + suf_mass * suf_factor
    summed = (pre_acc[:heads] + pre_acc[heads:]) * pre_factor + suf_acc * suf_factor
    own_rows = pl.ds(pl.multiple_of((y * NZ + z) * heads, heads), heads)
    attn_buf[own_rows, :] = (summed / total).astype(jnp.bfloat16)

    for a, b in WIDE:
        pltpu.make_async_remote_copy(
            attn_buf.at[own_rows],
            attn_buf.at[own_rows],
            attn_send,
            attn_recv,
            device_id=wide_at(a, b),
            device_id_type=MESH,
        ).start()
    swaps[2].wait_recv()
    landed(attn_buf.at[pl.ds(0, (CHIPS - 1) * heads)], attn_recv)

    attn32[...] = attn_buf[...].astype(jnp.float32)
    columns = w_hbm.shape[1]
    sums = [jnp.zeros((CHIPS, columns), jnp.float32) for _ in range(2)]
    for h in range(0, heads, 2):
        pair = jnp.concatenate(
            [attn32[pl.ds(h + i, CHIPS, stride=heads), :] for i in range(2)], axis=1
        ).astype(jnp.bfloat16)
        for d in range(2):
            sums[d] = sums[d] + jnp.dot(
                pair, wbuf[d, h * hd : (h + 2) * hd, :], preferred_element_type=jnp.float32
            )
    share = CHIPS // (NX * NL)
    for d in range(2):
        for t in range(NX * NL):
            part = sums[d][t * share : (t + 1) * share]
            proj_out[d, t] = jnp.concatenate([part[:, :128], part[:, 128:]], axis=0)
    for i, (a, b, d) in enumerate(TP):
        target = tp_at(a, b, d)
        pltpu.make_async_remote_copy(
            proj_out.at[d, target[1]],
            proj_in.at[i],
            proj_send,
            proj_recv,
            device_id=target,
            device_id_type=MESH,
        ).start()
    landed(proj_in, proj_recv)
    parts = [proj_out[0, tp], jnp.zeros((8, 128), jnp.float32)]
    for i, (a, b, d) in enumerate(TP):
        parts[d] = parts[d] + proj_in[i]
    for core in range(2):
        half = jnp.where(c == core, parts[0], parts[1])
        for i in range(share):
            for j in range(2):
                o_ref[2 * i + core : 2 * i + core + 1, j * 128 : (j + 1) * 128] = half[
                    j * share + i : j * share + i + 1
                ]

    landed(qbuf.at[pl.ds(0, NY - 1)], q_send)
    landed(qbuf.at[0, pl.ds(heads, rows - heads)], q_send)
    for swap in swaps:
        swap.wait_send()
    landed(acc_out.at[pl.ds(0, NY - 1)], acc_send)
    landed(acc_out.at[0, pl.ds(heads, rows - heads)], acc_send)
    landed(st_in.at[pl.ds(0, NY - 1)], st_send)
    landed(st_in.at[0, pl.ds(1, NZ - 1)], st_send)
    landed(attn_buf.at[pl.ds(0, (CHIPS - 1) * heads)], attn_send)
    landed(proj_in, proj_send)


def local(
    queries,
    new_keys,
    new_values,
    prefix_keys,
    prefix_values,
    suffix_keys,
    suffix_values,
    lengths,
    page_table,
    out_weight,
):
    _, heads, hd = queries.shape
    tokens = prefix_keys.shape[0] * prefix_keys.shape[1]
    slots = suffix_keys.shape[1]
    depth, columns = out_weight.shape
    rows = NZ * heads
    bf16, f32 = jnp.bfloat16, jnp.float32
    dma = pltpu.SemaphoreType.DMA
    return pl.pallas_call(
        kernel,
        out_shape=jax.ShapeDtypeStruct((8, columns), f32),
        in_specs=[pl.BlockSpec(memory_space=pltpu.SMEM)] + [pl.BlockSpec(memory_space=pl.ANY)] * 9,
        out_specs=pl.BlockSpec(memory_space=pltpu.VMEM),
        scratch_shapes=[
            pltpu.VMEM((NY, rows, hd), bf16),
            pltpu.VMEM((2, tokens, hd), bf16),
            pltpu.VMEM((2, tokens, hd), bf16),
            pltpu.VMEM((hd, 2 * tokens), bf16),
            pltpu.VMEM((slots, hd), bf16),
            pltpu.VMEM((slots, hd), bf16),
            pltpu.VMEM((1, hd), bf16),
            pltpu.VMEM((1, hd), bf16),
            pltpu.VMEM((1, page_table.shape[0]), jnp.int32),
            pltpu.VMEM((2, depth, columns), bf16),
            pltpu.VMEM((NY, rows, hd), bf16),
            pltpu.VMEM((NY, 2, rows), f32),
            pltpu.VMEM((NY, rows, hd), bf16),
            pltpu.VMEM((NY, NZ, 2, rows), f32),
            pltpu.VMEM((CHIPS * heads, hd), bf16),
            pltpu.VMEM((CHIPS * heads, hd), f32),
            pltpu.VMEM((2, NX * NL, 8, 128), f32),
            pltpu.VMEM((len(TP), 8, 128), f32),
            dma((9,)),
            dma,
            dma((NY,)),
            dma((3,)),
            dma((3,)),
            dma,
            dma((NY,)),
            dma,
            dma((NY,)),
            dma,
            dma,
            dma,
            dma,
        ],
        compiler_params=pltpu.CompilerParams(
            collective_id=0, has_side_effects=True, vmem_limit_bytes=32 * 1024 * 1024
        ),
        name="attention_step",
    )(
        lengths,
        queries.reshape(heads, hd),
        new_keys.reshape(1, hd),
        new_values.reshape(1, hd),
        prefix_keys.reshape(tokens, hd),
        prefix_values.reshape(tokens, hd),
        suffix_keys.reshape(slots, hd),
        suffix_values.reshape(slots, hd),
        page_table.reshape(1, -1),
        out_weight,
    )


def solution(mesh):
    in_specs = (
        P("wide", "tp", None),
        P("wide", "tp", None),
        P("wide", "tp", None),
        P("wide", None, "tp", None),
        P("wide", None, "tp", None),
        P("wide", None, "tp", None),
        P("wide", None, "tp", None),
        P("wide"),
        P(),
        P("tp", "wide"),
    )
    out_specs = P("tp", "wide")
    return jax.shard_map(local, mesh=mesh, in_specs=in_specs, out_specs=out_specs, check_vma=False)
```

time: 553 us -> 52.1 us (0.09); the launches traced: 545 us -> 51.9 us
  blocking collectives: 343 us -> 0 us
  other arithmetic: 94.4 us -> 0 us
  waiting for transfers between devices: 74.1 us -> 0 us
  Pallas kernels: 0 us -> 45 us
  between operations: 14.2 us -> 0.7 us
  local copies, waits for them, and re-layouts: 12.1 us -> 6.11 us
    all_gather x4 -> x0, blocking collectives: 343 us -> none  [the longest x2 170 us: joined_2(): gathered = jax.tree.map(lambda a: lax.all_gather(a, axis), part)]
    add x64 -> x0, other arithmetic: 90.5 us -> none  [the longest x63 90.5 us: combine_partials(): acc_one * factor_one[..., None] + acc_two * factor_two[..., None]]
    pallas_call x0 -> x1, Pallas kernels: none -> 45 us  [local(): pl.pallas_call(kernel, out_shape=jax.ShapeDtypeStruct((8, columns), f32),...]
    all_gather x1 -> x0, waiting for transfers between devices: 40 us -> none  [joined_2(): gathered = jax.tree.map(lambda a: lax.all_gather(a, axis), part)]
    reduce_scatter x1 -> x0, waiting for transfers between devices: 34.1 us -> none  [local(): return lax.psum_scatter(terms, 'tp', scatter_dimension=0, tiled=True)]
    mul x126 -> x0, local copies, waits for them, and re-layouts: 10.4 us -> none  [the longest x63 5.24 us: combine_partials(): acc_two * factor_two[..., None]]
    unnamed x15 -> x19, local copies, waits for them, and re-layouts: 0.21 us -> 6.11 us
  transfers between devices with their start and end apart: 2 -> 0, of which waited for: 2 -> 0; matrix products, arithmetic and copies ran while one was open for 0% -> 0% of each run, Pallas kernels for 0% -> 0%
where the time goes in v1:
time: 52.1 us; the launch traced here: 51.9 us
  Pallas kernels  45 us (86%)
  local copies, waits for them, and re-layouts  6.11 us (12%)
  between operations  0.7 us (1%)
    pallas_call x1, Pallas kernels, local(): pl.pallas_call(kernel, out_shape=jax.ShapeDtypeStruct((8, columns), f32),...  45 us
    unnamed x19, local copies, waits for them, and re-layouts  6.11 us

profile of v1, /device:TPU:1, one launch (start us, length us, event | category | flops | bytes accessed | tf_op | source)
XLA Modules:
  0.0 51.9 jit_solution(13612606592534144281)
XLA Ops:
  0.7 0.0 copy-start.5
  0.7 0.0 copy-start.6
  0.7 0.0 copy-start.7
  0.7 0.0 copy-start.8
  0.7 0.6 %copy-done.5 = bf16[1,16,128]{2,1,0:T(8,128)(2,1)S(1)} copy-done((bf16[1,16,128]{2,1,0:T(8,128)(2,1)S(1)}, bf16[1,16,128]{2,1,0:T(8,128)(2,1)}, u32[]{:S(2)}) %copy-start.5) | copy-done | bytes 4120
  1.3 0.0 copy-done.6
  1.3 0.0 copy-done.7
  1.3 0.0 copy-done.8
  1.4 0.0 copy-start
  1.4 1.2 %copy-done = bf16[2048,256]{1,0:T(8,128)(2,1)S(1)} copy-done((bf16[2048,256]{1,0:T(8,128)(2,1)S(1)}, bf16[2048,256]{1,0:T(8,128)(2,1)}, u32[]{:S(2)}) %copy-start) | copy-done | bytes 1048600
  2.6 0.0 copy-start.1
  2.6 0.9 %copy-done.1 = bf16[4,128,1,128]{3,1,2,0:T(8,128)(2,1)S(1)} copy-done((bf16[4,128,1,128]{3,1,2,0:T(8,128)(2,1)S(1)}, bf16[4,128,1,128]{3,1,2,0:T(8,128)(2,1)}, u32[]{:S(2)}) %copy-start.1) | copy-done | bytes 131096
  3.5 0.0 copy-start.2
  3.5 0.9 %copy-done.2 = bf16[4,128,1,128]{3,1,2,0:T(8,128)(2,1)S(1)} copy-done((bf16[4,128,1,128]{3,1,2,0:T(8,128)(2,1)S(1)}, bf16[4,128,1,128]{3,1,2,0:T(8,128)(2,1)}, u32[]{:S(2)}) %copy-start.2) | copy-done | bytes 131096
  4.4 0.0 copy-start.3
  4.4 0.9 %copy-done.3 = bf16[1,512,1,128]{3,1,2,0:T(8,128)(2,1)S(1)} copy-done((bf16[1,512,1,128]{3,1,2,0:T(8,128)(2,1)S(1)}, bf16[1,512,1,128]{3,1,2,0:T(8,128)(2,1)}, u32[]{:S(2)}) %copy-start.3) | copy-done | bytes 131096
  5.3 0.0 copy-start.4
  5.3 0.9 %copy-done.4 = bf16[1,512,1,128]{3,1,2,0:T(8,128)(2,1)S(1)} copy-done((bf16[1,512,1,128]{3,1,2,0:T(8,128)(2,1)S(1)}, bf16[1,512,1,128]{3,1,2,0:T(8,128)(2,1)}, u32[]{:S(2)}) %copy-start.4) | copy-done | bytes 131096
  6.2 45.0 %attention_step.1 = f32[8,256]{1,0:T(8,128)S(1)} custom-call(s32[1]{0:T(128)S(6)} %copy.12.len_ref, bf16[16,128]{1,0:T(8,128)(2,1)S(1)} %bitcast.12, bf16[1,128]{1,0:T(2,128)(2,1)S(1)} %bitcast.13, bf16[1,128]{1,0:T(2,128)(2,1)S(1)} %bitcast.14, bf16[512,128]{1,0:T(8,128)(2,1)S(1)} %bitcast.8, bf16[512,128]{1,0:T(8,128)(2,1)S(1)} %bitcast.9, ...), custom_call_target="tpu_custom_call" | custom-call | tf_op jit(solution)/shard_map/attention_step/pallas_call | solution.py:321
  51.3 0.6 %copy.13 = f32[8,256]{1,0:T(8,128)} copy(f32[8,256]{1,0:T(8,128)S(1)} %attention_step.1) | data formatting | bytes 16384
Async XLA Ops:
  0.7 0.7 %copy-start.5 = (bf16[1,16,128]{2,1,0:T(8,128)(2,1)S(1)}, bf16[1,16,128]{2,1,0:T(8,128)(2,1)}, u32[]{:S(2)}) copy-start(bf16[1,16,128]{2,1,0:T(8,128)(2,1)} %param.10) | copy-start | bytes 12292
  0.7 0.7 %copy-start.6 = (bf16[1,1,128]{2,1,0:T(2,128)(2,1)S(1)}, bf16[1,1,128]{2,1,0:T(2,128)(2,1)}, u32[]{:S(2)}) copy-start(bf16[1,1,128]{2,1,0:T(2,128)(2,1)} %param.11) | copy-start | bytes 772
  0.7 0.7 %copy-start.7 = (bf16[1,1,128]{2,1,0:T(2,128)(2,1)S(1)}, bf16[1,1,128]{2,1,0:T(2,128)(2,1)}, u32[]{:S(2)}) copy-start(bf16[1,1,128]{2,1,0:T(2,128)(2,1)} %param.12) | copy-start | bytes 772
  0.7 0.7 %copy-start.8 = (s32[128]{0:T(128)S(1)}, s32[128]{0:T(128)}, u32[]{:S(2)}) copy-start(s32[128]{0:T(128)} %param.18) | copy-start | bytes 1540
  1.4 1.2 %copy-start = (bf16[2048,256]{1,0:T(8,128)(2,1)S(1)}, bf16[2048,256]{1,0:T(8,128)(2,1)}, u32[]{:S(2)}) copy-start(bf16[2048,256]{1,0:T(8,128)(2,1)} %w_hbm.1) | copy-start | bytes 3145732
  2.6 0.9 %copy-start.1 = (bf16[4,128,1,128]{3,1,2,0:T(8,128)(2,1)S(1)}, bf16[4,128,1,128]{3,1,2,0:T(8,128)(2,1)}, u32[]{:S(2)}) copy-start(bf16[4,128,1,128]{3,1,2,0:T(8,128)(2,1)} %param.13) | copy-start | bytes 393220
  3.5 0.9 %copy-start.2 = (bf16[4,128,1,128]{3,1,2,0:T(8,128)(2,1)S(1)}, bf16[4,128,1,128]{3,1,2,0:T(8,128)(2,1)}, u32[]{:S(2)}) copy-start(bf16[4,128,1,128]{3,1,2,0:T(8,128)(2,1)} %param.14) | copy-start | bytes 393220
  4.4 0.9 %copy-start.3 = (bf16[1,512,1,128]{3,1,2,0:T(8,128)(2,1)S(1)}, bf16[1,512,1,128]{3,1,2,0:T(8,128)(2,1)}, u32[]{:S(2)}) copy-start(bf16[1,512,1,128]{3,1,2,0:T(8,128)(2,1)} %param.15) | copy-start | bytes 393220
  5.3 0.9 %copy-start.4 = (bf16[1,512,1,128]{3,1,2,0:T(8,128)(2,1)S(1)}, bf16[1,512,1,128]{3,1,2,0:T(8,128)(2,1)}, u32[]{:S(2)}) copy-start(bf16[1,512,1,128]{3,1,2,0:T(8,128)(2,1)} %param.16) | copy-start | bytes 393220

commit v2 on v1

--- a/solution.py
+++ b/solution.py
@@ -101,12 +101,11 @@
         load.wait()
 
     own_q = qbuf[0, :heads]
-    length = len_ref[0]
     slots = skbuf.shape[0]
     scores = lax.dot_general(
         own_q, skbuf[...], (((1,), (1,)), ((), ())), preferred_element_type=jnp.float32
     )
-    live = lax.broadcasted_iota(jnp.int32, (heads, slots), 1) < length
+    live = lax.broadcasted_iota(jnp.int32, (heads, slots), 1) < len_ref[0]
     scores = jnp.where(live, scores, -1e30)
     new_score = jnp.sum(
         own_q.astype(jnp.float32) * nkbuf[...].astype(jnp.float32), axis=1, keepdims=True
@@ -320,7 +319,7 @@
     dma = pltpu.SemaphoreType.DMA
     return pl.pallas_call(
         kernel,
-        out_shape=jax.ShapeDtypeStruct((8, columns), f32),
+        out_shape=pltpu.VMEM((8, columns), f32),
         in_specs=[pl.BlockSpec(memory_space=pltpu.SMEM)] + [pl.BlockSpec(memory_space=pl.ANY)] * 9,
         out_specs=pl.BlockSpec(memory_space=pltpu.VMEM),
         scratch_shapes=[
@@ -362,15 +361,20 @@
         name="attention_step",
     )(
         lengths,
-        queries.reshape(heads, hd),
-        new_keys.reshape(1, hd),
-        new_values.reshape(1, hd),
-        prefix_keys.reshape(tokens, hd),
-        prefix_values.reshape(tokens, hd),
-        suffix_keys.reshape(slots, hd),
-        suffix_values.reshape(slots, hd),
-        page_table.reshape(1, -1),
-        out_weight,
+        *(
+            pltpu.with_memory_space_constraint(a, pltpu.HBM)
+            for a in (
+                queries.reshape(heads, hd),
+                new_keys.reshape(1, hd),
+                new_values.reshape(1, hd),
+                prefix_keys.reshape(tokens, hd),
+                prefix_values.reshape(tokens, hd),
+                suffix_keys.reshape(slots, hd),
+                suffix_values.reshape(slots, hd),
+                page_table.reshape(1, -1),
+                out_weight,
+            )
+        ),
     )
 
 

time: 52.1 us -> 46.3 us (0.89)
  local copies, waits for them, and re-layouts: 6.11 us -> 0.6 us
    unnamed x19 -> x1, local copies, waits for them, and re-layouts: 6.11 us -> 0.6 us
where the time goes in v2:
time: 46.3 us; the launch traced here: 46.2 us
  Pallas kernels  44.9 us (97%)
  between operations  0.66 us (1%)
  local copies, waits for them, and re-layouts  0.6 us (1%)
    pallas_call x1, Pallas kernels, local(): pl.pallas_call(kernel, out_shape=pltpu.VMEM((8, columns), f32), in_specs=...  44.9 us

profile of v2, /device:TPU:1, one launch (start us, length us, event | category | flops | bytes accessed | tf_op | source)
XLA Modules:
  0.0 46.2 jit_solution(2724224011040905173)
XLA Ops:
  0.7 44.9 %attention_step.1 = f32[8,256]{1,0:T(8,128)S(1)} custom-call(s32[1]{0:T(128)S(6)} %copy.13.len_ref, bf16[16,128]{1,0:T(8,128)(2,1)} %bitcast.12, bf16[1,128]{1,0:T(2,128)(2,1)} %bitcast.13, bf16[1,128]{1,0:T(2,128)(2,1)} %bitcast.14, bf16[512,128]{1,0:T(8,128)(2,1)} %bitcast.8, bf16[512,128]{1,0:T(8,128)(2,1)} %bitcast.9, bf16[512,128]{1,0:T(8,128)(2,1)} %bitcast.10, ...), custom_call_target="tpu_custom_call" | custom-call | tf_op jit(solution)/shard_map/attention_step/pallas_call | solution.py:320
  45.6 0.6 %copy.12 = f32[8,256]{1,0:T(8,128)} copy(f32[8,256]{1,0:T(8,128)S(1)} %attention_step.1) | data formatting | bytes 16384

commit v3 on v2

--- a/solution.py
+++ b/solution.py
@@ -13,6 +13,7 @@
 CHIPS = NY * NZ
 WIDE = [(a, b) for a in (2, 1, 3, 0) for b in (4, 3, 5, 2, 6, 1, 7, 0) if (a, b) != (0, 0)]
 TP = [(a, b, d) for a in (2, 1, 3, 0) for b in (1, 0) for d in (1, 0) if (a, b, d) != (0, 0, 0)]
+GROUPS = ((0,), (1, 3), (2,))
 LOG2E = 1.4426950408889634
 
 
@@ -91,7 +92,7 @@
         (nv_hbm, nvbuf),
         (pt_hbm, ptbuf),
         (pk_hbm, kbuf.at[0]),
-        (pv_hbm, vbuf.at[0]),
+        (pv_hbm, vbuf.at[0, :, pl.ds(0, hd)]),
         (w_hbm, wbuf.at[0]),
     ]
     loads = [pltpu.make_async_copy(src, dst, local_sem.at[i]) for i, (src, dst) in enumerate(loads)]
@@ -132,6 +133,7 @@
     for load in loads[6:]:
         load.wait()
     ktbuf[:, :tokens] = kbuf[0].T
+    vbuf[:, :, hd:] = jnp.ones((2, tokens, hd), jnp.bfloat16)
 
     pl.semaphore_wait(barrier, len(WIDE) + len(TP))
 
@@ -146,36 +148,47 @@
         ).start()
     swaps = [
         pltpu.make_async_remote_copy(
-            buf.at[0],
-            buf.at[1],
+            src,
+            dst,
             core_send.at[i],
             core_recv.at[i],
             device_id=partner,
             device_id_type=MESH,
         )
-        for i, buf in enumerate((kbuf, vbuf, wbuf))
+        for i, (src, dst) in enumerate(
+            (
+                (kbuf.at[0], kbuf.at[1]),
+                (vbuf.at[0, :, pl.ds(0, hd)], vbuf.at[1, :, pl.ds(0, hd)]),
+                (wbuf.at[0], wbuf.at[1]),
+            )
+        )
     ]
     for swap in swaps:
         swap.start()
     swaps[0].wait_recv()
     ktbuf[:, tokens:] = kbuf[1].T
     swaps[1].wait_recv()
-    values = vbuf[...].reshape(2 * tokens, hd)
+    values = vbuf[...].reshape(2 * tokens, 2 * hd)
 
     def landed(ref, sem):
         pltpu.make_async_copy(ref, ref, sem).wait()
 
-    lane = lax.broadcasted_iota(jnp.int32, (rows, 128), 1)
-    for a in (0, 1, 3, 2):
-        landed(qbuf.at[0, pl.ds(heads, rows - heads)] if a == 0 else qbuf.at[a], q_recv.at[a])
+    diagonal = lax.broadcasted_iota(jnp.int32, (rows, 128), 0) == lax.broadcasted_iota(
+        jnp.int32, (rows, 128), 1
+    )
+
+    def line(column):
+        return jnp.sum(jnp.where(diagonal, column, 0.0), axis=0, keepdims=True)
+
+    def chunk(a):
         s = jnp.dot(qbuf[a], ktbuf[...], preferred_element_type=jnp.float32) + bias
         top = jnp.max(s, axis=1, keepdims=True)
-        p = jnp.exp2((s - top) * scale)
-        mass = jnp.sum(p, axis=1, keepdims=True)
-        acc = jnp.dot(p.astype(jnp.bfloat16), values, preferred_element_type=jnp.float32)
-        acc_out[a] = acc.astype(jnp.bfloat16)
-        stats = jnp.where(lane == 0, top * scale, jnp.where(lane == 1, mass, 0.0))
-        st_out[a] = stats.T[:2]
+        p = jnp.exp2((s - top) * scale).astype(jnp.bfloat16)
+        acc = jnp.dot(p, values, preferred_element_type=jnp.float32)
+        acc_out[a] = acc[:, :hd].astype(jnp.bfloat16)
+        st_out[a] = jnp.concatenate([line(top * scale), line(acc[:, hd:])], axis=0)
+
+    def reply(a):
         for b in (4, 3, 5, 2, 6, 1, 7, 0):
             if (a, b) == (0, 0):
                 continue
@@ -199,40 +212,43 @@
             acc_in[0, :heads] = acc_out[0, :heads]
             st_in[0, 0] = st_out[0]
 
+    for group in GROUPS:
+        for a in group:
+            landed(qbuf.at[0, pl.ds(heads, rows - heads)] if a == 0 else qbuf.at[a], q_recv.at[a])
+        for a in group:
+            chunk(a)
+        for a in group:
+            reply(a)
+
     spot = lax.broadcasted_iota(jnp.int32, (2, rows), 1) // heads
     joined = []
     for a in range(NY):
         landed(st_in.at[0, pl.ds(1, NZ - 1)] if a == 0 else st_in.at[a], st_recv.at[a])
-        line = jnp.zeros((2, rows), jnp.float32)
-        for b in range(NZ):
-            line = jnp.where(spot == b, st_in[a, b], line)
-        joined.append(line)
-    tops = jnp.concatenate([line[:1] for line in joined], axis=0)
-    masses = jnp.concatenate([line[1:] for line in joined], axis=0)
-    best = jnp.broadcast_to(jnp.max(tops, axis=0, keepdims=True), (8, rows))
-    for shift in (heads, 2 * heads, 4 * heads):
-        best = jnp.maximum(best, pltpu.roll(best, shift, 1))
-    factors = jnp.exp2(tops - best[:1])
-    mass_line = jnp.sum(factors * masses, axis=0, keepdims=True)
+        both = st_in[a, 0]
+        for b in range(1, NZ):
+            both = jnp.where(spot == b, st_in[a, b], both)
+        joined.append(both)
+    best = functools.reduce(jnp.maximum, [both[:1] for both in joined])
     mine = lax.broadcasted_iota(jnp.int32, (heads, rows), 1) % heads == lax.broadcasted_iota(
         jnp.int32, (heads, rows), 0
     )
-    pre_max = jnp.max(jnp.where(mine, best[:1], -3e38), axis=1, keepdims=True)
-    pre_mass = jnp.sum(jnp.where(mine, mass_line, 0.0), axis=1, keepdims=True)
-    pre_acc = jnp.zeros((2 * heads, hd), jnp.float32)
+    row_max = jnp.maximum(
+        jnp.max(jnp.where(mine, best, -3e38), axis=1, keepdims=True), suf_max
+    )
+    spread = [jnp.where(mine, jnp.exp2(both[:1] - row_max), 0.0) for both in joined]
+    shares = functools.reduce(jnp.add, [f * both[1:] for f, both in zip(spread, joined)])
+    suf_factor = jnp.exp2(suf_max - row_max)
+    total = jnp.sum(shares, axis=1, keepdims=True) + suf_mass * suf_factor
+    spread = jnp.concatenate(spread, axis=1)
+    high = spread.astype(jnp.bfloat16)
+    rest = (spread - high.astype(jnp.float32)).astype(jnp.bfloat16)
+    factors = jnp.concatenate([high, rest], axis=0)
     for a in range(NY):
-        spread = jnp.where(mine, factors[a : a + 1], 0.0)
-        high = spread.astype(jnp.bfloat16)
-        rest = (spread - high.astype(jnp.float32)).astype(jnp.bfloat16)
         landed(acc_in.at[0, pl.ds(heads, rows - heads)] if a == 0 else acc_in.at[a], acc_recv.at[a])
-        pre_acc = pre_acc + jnp.dot(
-            jnp.concatenate([high, rest], axis=0), acc_in[a], preferred_element_type=jnp.float32
-        )
-    row_max = jnp.maximum(pre_max, suf_max)
-    pre_factor = jnp.exp2(pre_max - row_max)
-    suf_factor = jnp.exp2(suf_max - row_max)
-    total = pre_mass * pre_factor + suf_mass * suf_factor
-    summed = (pre_acc[:heads] + pre_acc[heads:]) * pre_factor + suf_acc * suf_factor
+    pre_acc = jnp.dot(
+        factors, acc_in[...].reshape(NY * rows, hd), preferred_element_type=jnp.float32
+    )
+    summed = pre_acc[:heads] + pre_acc[heads:] + suf_acc * suf_factor
     own_rows = pl.ds(pl.multiple_of((y * NZ + z) * heads, heads), heads)
     attn_buf[own_rows, :] = (summed / total).astype(jnp.bfloat16)
 
@@ -241,14 +257,16 @@
             attn_buf.at[own_rows],
             attn_buf.at[own_rows],
             attn_send,
-            attn_recv,
+            attn_recv.at[a],
             device_id=wide_at(a, b),
             device_id_type=MESH,
         ).start()
     swaps[2].wait_recv()
-    landed(attn_buf.at[pl.ds(0, (CHIPS - 1) * heads)], attn_recv)
-
-    attn32[...] = attn_buf[...].astype(jnp.float32)
+    for a in (0, 1, 3, 2):
+        block = pl.ds(pl.multiple_of((y - a + NY) % NY * rows, rows), rows)
+        landed(attn_buf.at[pl.ds(0, rows - heads if a == 0 else rows)], attn_recv.at[a])
+        attn32[block, :] = attn_buf[block, :].astype(jnp.float32)
+
     columns = w_hbm.shape[1]
     sums = [jnp.zeros((CHIPS, columns), jnp.float32) for _ in range(2)]
     for h in range(0, heads, 2):
@@ -325,7 +343,7 @@
         scratch_shapes=[
             pltpu.VMEM((NY, rows, hd), bf16),
             pltpu.VMEM((2, tokens, hd), bf16),
-            pltpu.VMEM((2, tokens, hd), bf16),
+            pltpu.VMEM((2, tokens, 2 * hd), bf16),
             pltpu.VMEM((hd, 2 * tokens), bf16),
             pltpu.VMEM((slots, hd), bf16),
             pltpu.VMEM((slots, hd), bf16),
@@ -351,7 +369,7 @@
             dma,
             dma((NY,)),
             dma,
-            dma,
+            dma((NY,)),
             dma,
             dma,
         ],

time: 46.3 us -> 46 us (level)
  no operation moved by 1% of the time
where the time goes in v3:
time: 46 us; the launch traced here: 45.8 us
  Pallas kernels  44.6 us (97%)
  between operations  0.66 us (1%)
  local copies, waits for them, and re-layouts  0.6 us (1%)
    pallas_call x1, Pallas kernels, local(): pl.pallas_call(kernel, out_shape=pltpu.VMEM((8, columns), f32), in_specs=...  44.6 us

profile of v3, /device:TPU:1, one launch (start us, length us, event | category | flops | bytes accessed | tf_op | source)
XLA Modules:
  0.0 45.8 jit_solution(14351706684171844907)
XLA Ops:
  0.7 44.6 %attention_step.1 = f32[8,256]{1,0:T(8,128)S(1)} custom-call(s32[1]{0:T(128)S(6)} %copy.13.len_ref, bf16[16,128]{1,0:T(8,128)(2,1)} %bitcast.12, bf16[1,128]{1,0:T(2,128)(2,1)} %bitcast.13, bf16[1,128]{1,0:T(2,128)(2,1)} %bitcast.14, bf16[512,128]{1,0:T(8,128)(2,1)} %bitcast.8, bf16[512,128]{1,0:T(8,128)(2,1)} %bitcast.9, bf16[512,128]{1,0:T(8,128)(2,1)} %bitcast.10, ...), custom_call_target="tpu_custom_call" | custom-call | tf_op jit(solution)/shard_map/attention_step/pallas_call | solution.py:338
  45.2 0.6 %copy.12 = f32[8,256]{1,0:T(8,128)} copy(f32[8,256]{1,0:T(8,128)S(1)} %attention_step.1) | data formatting | bytes 16384

commit v4 on v3

--- a/solution.py
+++ b/solution.py
@@ -257,41 +257,62 @@
             attn_buf.at[own_rows],
             attn_buf.at[own_rows],
             attn_send,
-            attn_recv.at[a],
+            attn_recv.at[y],
             device_id=wide_at(a, b),
             device_id_type=MESH,
         ).start()
     swaps[2].wait_recv()
-    for a in (0, 1, 3, 2):
-        block = pl.ds(pl.multiple_of((y - a + NY) % NY * rows, rows), rows)
-        landed(attn_buf.at[pl.ds(0, rows - heads if a == 0 else rows)], attn_recv.at[a])
+    def rows_of(plane):
+        sem = attn_recv.at[plane]
+        pl.when(y == plane)(lambda: landed(attn_buf.at[pl.ds(0, rows - heads)], sem))
+        pl.when(y != plane)(lambda: landed(attn_buf.at[pl.ds(0, rows)], sem))
+        block = slice(plane * rows, (plane + 1) * rows)
         attn32[block, :] = attn_buf[block, :].astype(jnp.float32)
 
     columns = w_hbm.shape[1]
-    sums = [jnp.zeros((CHIPS, columns), jnp.float32) for _ in range(2)]
-    for h in range(0, heads, 2):
-        pair = jnp.concatenate(
-            [attn32[pl.ds(h + i, CHIPS, stride=heads), :] for i in range(2)], axis=1
-        ).astype(jnp.bfloat16)
+    share = CHIPS // (NX * NL)
+
+    def project(first, count):
+        sums = [jnp.zeros((count, columns), jnp.float32) for _ in range(2)]
+        for h in range(0, heads, 2):
+            pair = jnp.concatenate(
+                [
+                    attn32[pl.ds(first * heads + h + i, count, stride=heads), :]
+                    for i in range(2)
+                ],
+                axis=1,
+            ).astype(jnp.bfloat16)
+            for d in range(2):
+                sums[d] = sums[d] + jnp.dot(
+                    pair, wbuf[d, h * hd : (h + 2) * hd, :], preferred_element_type=jnp.float32
+                )
         for d in range(2):
-            sums[d] = sums[d] + jnp.dot(
-                pair, wbuf[d, h * hd : (h + 2) * hd, :], preferred_element_type=jnp.float32
+            for t in range(count // share):
+                part = sums[d][t * share : (t + 1) * share]
+                proj_out[d, first // share + t] = jnp.concatenate(
+                    [part[:, :128], part[:, 128:]], axis=0
+                )
+
+    def send_sums(wanted):
+        for i, (a, b, d) in enumerate(TP):
+            target = tp_at(a, b, d)
+            copy = pltpu.make_async_remote_copy(
+                proj_out.at[d, target[1]],
+                proj_in.at[i],
+                proj_send,
+                proj_recv,
+                device_id=target,
+                device_id_type=MESH,
             )
-    share = CHIPS // (NX * NL)
-    for d in range(2):
-        for t in range(NX * NL):
-            part = sums[d][t * share : (t + 1) * share]
-            proj_out[d, t] = jnp.concatenate([part[:, :128], part[:, 128:]], axis=0)
-    for i, (a, b, d) in enumerate(TP):
-        target = tp_at(a, b, d)
-        pltpu.make_async_remote_copy(
-            proj_out.at[d, target[1]],
-            proj_in.at[i],
-            proj_send,
-            proj_recv,
-            device_id=target,
-            device_id_type=MESH,
-        ).start()
+            pl.when(wanted((x + a) % NX))(copy.start)
+
+    rows_of(0)
+    project(0, NZ)
+    send_sums(lambda to: to == 0)
+    for plane in range(1, NY):
+        rows_of(plane)
+    project(NZ, CHIPS - NZ)
+    send_sums(lambda to: to != 0)
     landed(proj_in, proj_recv)
     parts = [proj_out[0, tp], jnp.zeros((8, 128), jnp.float32)]
     for i, (a, b, d) in enumerate(TP):

time: 46 us -> 44.2 us (0.961)
  Pallas kernels: 44.6 us -> 42.6 us
    pallas_call x1, Pallas kernels: 44.6 us -> 42.6 us  [local(): pl.pallas_call(kernel, out_shape=pltpu.VMEM((8, columns), f32), in_specs=...]
where the time goes in v4:
time: 44.2 us; the launch traced here: 43.9 us
  Pallas kernels  42.6 us (96%)
  between operations  0.66 us (1%)
  local copies, waits for them, and re-layouts  0.6 us (1%)
    pallas_call x1, Pallas kernels, local(): pl.pallas_call(kernel, out_shape=pltpu.VMEM((8, columns), f32), in_specs=...  42.6 us

profile of v4, /device:TPU:1, one launch (start us, length us, event | category | flops | bytes accessed | tf_op | source)
XLA Modules:
  0.0 43.9 jit_solution(4775174946639629705)
XLA Ops:
  0.7 42.6 %attention_step.1 = f32[8,256]{1,0:T(8,128)S(1)} custom-call(s32[1]{0:T(128)S(6)} %copy.13.len_ref, bf16[16,128]{1,0:T(8,128)(2,1)} %bitcast.12, bf16[1,128]{1,0:T(2,128)(2,1)} %bitcast.13, bf16[1,128]{1,0:T(2,128)(2,1)} %bitcast.14, bf16[512,128]{1,0:T(8,128)(2,1)} %bitcast.8, bf16[512,128]{1,0:T(8,128)(2,1)} %bitcast.9, bf16[512,128]{1,0:T(8,128)(2,1)} %bitcast.10, ...), custom_call_target="tpu_custom_call" | custom-call | tf_op jit(solution)/shard_map/attention_step/pallas_call | solution.py:359
  43.3 0.6 %copy.12 = f32[8,256]{1,0:T(8,128)} copy(f32[8,256]{1,0:T(8,128)S(1)} %attention_step.1) | data formatting | bytes 16384

commit v5 on v4

--- a/solution.py
+++ b/solution.py
@@ -43,6 +43,8 @@
     st_out,
     acc_in,
     st_in,
+    suf_out,
+    suf_in,
     attn_buf,
     attn32,
     proj_out,
@@ -56,6 +58,8 @@
     acc_recv,
     st_send,
     st_recv,
+    suf_send,
+    suf_recv,
     attn_send,
     attn_recv,
     proj_send,
@@ -70,8 +74,16 @@
     y, z, c = wide // (2 * NZ), (wide // 2) % NZ, wide % 2
     x, low = tp // NL, tp % NL
 
-    def wide_at(a, b, sign=1):
-        return (((y + sign * a + NY) % NY) * (2 * NZ) + ((z + sign * b + NZ) % NZ) * 2 + c, tp)
+    def wide_at(a, b):
+        return (((y + a) % NY) * (2 * NZ) + ((z + b) % NZ) * 2 + c, tp)
+
+    def join_at(a, b):
+        of_y, of_z = (y - a + NY) % NY, (z - b + NZ) % NZ
+        return (of_z // 2 * (2 * NZ) + (of_y + of_z % 2 * (NZ - 1 - 2 * of_y)) * 2 + c, tp)
+
+    join_y, join_z = z + z // NY * (NZ - 1 - 2 * z), 2 * y + z // NY
+    suffix_to = join_at(0, 0)
+    moved = suffix_to[0] != wide
 
     def tp_at(a, b, d):
         return (wide - c + (c + d) % 2, ((x + a) % NX) * NL + (low + b) % NL)
@@ -119,7 +131,10 @@
     suf_acc = suf_acc + new_weight.astype(jnp.bfloat16).astype(jnp.float32) * nvbuf[...].astype(
         jnp.float32
     )
-    suf_max = suf_max * scale
+    suf_out[:heads] = suf_acc
+    suf_out[heads:] = jnp.where(
+        lax.broadcasted_iota(jnp.int32, (heads, hd), 1) == 0, suf_max * scale, suf_mass
+    )
 
     pages = tokens // 128
     bias = []
@@ -146,6 +161,20 @@
             device_id=wide_at(a, b),
             device_id_type=MESH,
         ).start()
+    suffix = pltpu.make_async_remote_copy(
+        suf_out,
+        suf_in,
+        suf_send,
+        suf_recv,
+        device_id=suffix_to,
+        device_id_type=MESH,
+    )
+    pl.when(moved)(suffix.start)
+
+    @pl.when(jnp.logical_not(moved))
+    def _():
+        suf_in[...] = suf_out[...]
+
     swaps = [
         pltpu.make_async_remote_copy(
             src,
@@ -190,27 +219,33 @@
 
     def reply(a):
         for b in (4, 3, 5, 2, 6, 1, 7, 0):
-            if (a, b) == (0, 0):
-                continue
-            pltpu.make_async_remote_copy(
-                st_out.at[a],
-                st_in.at[a, b],
-                st_send,
-                st_recv.at[a],
-                device_id=wide_at(a, b, -1),
-                device_id_type=MESH,
-            ).start()
-            pltpu.make_async_remote_copy(
-                acc_out.at[a, pl.ds(b * heads, heads)],
-                acc_in.at[a, pl.ds(b * heads, heads)],
-                acc_send,
-                acc_recv.at[a],
-                device_id=wide_at(a, b, -1),
-                device_id_type=MESH,
-            ).start()
-        if a == 0:
-            acc_in[0, :heads] = acc_out[0, :heads]
-            st_in[0, 0] = st_out[0]
+            target = join_at(a, b)
+            place = pl.ds(b * heads, heads)
+            into = pl.ds((a * NZ + b) * heads, heads)
+
+            @pl.when(target[0] != wide)
+            def _():
+                pltpu.make_async_remote_copy(
+                    st_out.at[a],
+                    st_in.at[a * NZ + b],
+                    st_send,
+                    st_recv,
+                    device_id=target,
+                    device_id_type=MESH,
+                ).start()
+                pltpu.make_async_remote_copy(
+                    acc_out.at[a, place],
+                    acc_in.at[into],
+                    acc_send,
+                    acc_recv,
+                    device_id=target,
+                    device_id_type=MESH,
+                ).start()
+
+            @pl.when(target[0] == wide)
+            def _():
+                st_in[a * NZ + b] = st_out[a]
+                acc_in[into, :] = acc_out[a, place, :]
 
     for group in GROUPS:
         for a in group:
@@ -222,11 +257,13 @@
 
     spot = lax.broadcasted_iota(jnp.int32, (2, rows), 1) // heads
     joined = []
+    landed(st_in.at[pl.ds(0, CHIPS - 1)], st_recv)
+    pl.when(moved)(lambda: landed(suf_in, suf_recv))
+    suf_acc, suf_max, suf_mass = suf_in[:heads], suf_in[heads:, :1], suf_in[heads:, 1:2]
     for a in range(NY):
-        landed(st_in.at[0, pl.ds(1, NZ - 1)] if a == 0 else st_in.at[a], st_recv.at[a])
-        both = st_in[a, 0]
+        both = st_in[a * NZ]
         for b in range(1, NZ):
-            both = jnp.where(spot == b, st_in[a, b], both)
+            both = jnp.where(spot == b, st_in[a * NZ + b], both)
         joined.append(both)
     best = functools.reduce(jnp.maximum, [both[:1] for both in joined])
     mine = lax.broadcasted_iota(jnp.int32, (heads, rows), 1) % heads == lax.broadcasted_iota(
@@ -243,29 +280,34 @@
     high = spread.astype(jnp.bfloat16)
     rest = (spread - high.astype(jnp.float32)).astype(jnp.bfloat16)
     factors = jnp.concatenate([high, rest], axis=0)
-    for a in range(NY):
-        landed(acc_in.at[0, pl.ds(heads, rows - heads)] if a == 0 else acc_in.at[a], acc_recv.at[a])
-    pre_acc = jnp.dot(
-        factors, acc_in[...].reshape(NY * rows, hd), preferred_element_type=jnp.float32
-    )
+    landed(acc_in.at[pl.ds(0, (CHIPS - 1) * heads)], acc_recv)
+    pre_acc = jnp.dot(factors, acc_in[...], preferred_element_type=jnp.float32)
     summed = pre_acc[:heads] + pre_acc[heads:] + suf_acc * suf_factor
-    own_rows = pl.ds(pl.multiple_of((y * NZ + z) * heads, heads), heads)
+    own_rows = pl.ds(pl.multiple_of((join_y * NZ + join_z) * heads, heads), heads)
     attn_buf[own_rows, :] = (summed / total).astype(jnp.bfloat16)
 
-    for a, b in WIDE:
+    def send_rows(device):
         pltpu.make_async_remote_copy(
             attn_buf.at[own_rows],
             attn_buf.at[own_rows],
             attn_send,
-            attn_recv.at[y],
-            device_id=wide_at(a, b),
+            attn_recv.at[join_y],
+            device_id=device,
             device_id_type=MESH,
         ).start()
+
+    for plane in (0, 1, 2, 3, 4, 5, 6, 7):
+        for a in (2, 1, 3, 0):
+            device = ((y + a) % NY * (2 * NZ) + plane * 2 + c, tp)
+            if a:
+                send_rows(device)
+            else:
+                pl.when(z != plane)(functools.partial(send_rows, device))
     swaps[2].wait_recv()
     def rows_of(plane):
         sem = attn_recv.at[plane]
-        pl.when(y == plane)(lambda: landed(attn_buf.at[pl.ds(0, rows - heads)], sem))
-        pl.when(y != plane)(lambda: landed(attn_buf.at[pl.ds(0, rows)], sem))
+        pl.when(join_y == plane)(lambda: landed(attn_buf.at[pl.ds(0, rows - heads)], sem))
+        pl.when(join_y != plane)(lambda: landed(attn_buf.at[pl.ds(0, rows)], sem))
         block = slice(plane * rows, (plane + 1) * rows)
         attn32[block, :] = attn_buf[block, :].astype(jnp.float32)
 
@@ -306,13 +348,14 @@
             )
             pl.when(wanted((x + a) % NX))(copy.start)
 
-    rows_of(0)
-    project(0, NZ)
-    send_sums(lambda to: to == 0)
-    for plane in range(1, NY):
+    for plane in range(2):
         rows_of(plane)
-    project(NZ, CHIPS - NZ)
-    send_sums(lambda to: to != 0)
+        project(plane * NZ, NZ)
+        send_sums(lambda to: to == plane)
+    for plane in range(2, NY):
+        rows_of(plane)
+    project(2 * NZ, CHIPS - 2 * NZ)
+    send_sums(lambda to: to > 1)
     landed(proj_in, proj_recv)
     parts = [proj_out[0, tp], jnp.zeros((8, 128), jnp.float32)]
     for i, (a, b, d) in enumerate(TP):
@@ -331,8 +374,8 @@
         swap.wait_send()
     landed(acc_out.at[pl.ds(0, NY - 1)], acc_send)
     landed(acc_out.at[0, pl.ds(heads, rows - heads)], acc_send)
-    landed(st_in.at[pl.ds(0, NY - 1)], st_send)
-    landed(st_in.at[0, pl.ds(1, NZ - 1)], st_send)
+    landed(st_in.at[pl.ds(0, CHIPS - 1)], st_send)
+    pl.when(moved)(suffix.wait_send)
     landed(attn_buf.at[pl.ds(0, (CHIPS - 1) * heads)], attn_send)
     landed(proj_in, proj_send)
 
@@ -374,8 +417,10 @@
             pltpu.VMEM((2, depth, columns), bf16),
             pltpu.VMEM((NY, rows, hd), bf16),
             pltpu.VMEM((NY, 2, rows), f32),
-            pltpu.VMEM((NY, rows, hd), bf16),
-            pltpu.VMEM((NY, NZ, 2, rows), f32),
+            pltpu.VMEM((CHIPS * heads, hd), bf16),
+            pltpu.VMEM((CHIPS, 2, rows), f32),
+            pltpu.VMEM((2 * heads, hd), f32),
+            pltpu.VMEM((2 * heads, hd), f32),
             pltpu.VMEM((CHIPS * heads, hd), bf16),
             pltpu.VMEM((CHIPS * heads, hd), f32),
             pltpu.VMEM((2, NX * NL, 8, 128), f32),
@@ -386,9 +431,11 @@
             dma((3,)),
             dma((3,)),
             dma,
-            dma((NY,)),
-            dma,
-            dma((NY,)),
+            dma,
+            dma,
+            dma,
+            dma,
+            dma,
             dma,
             dma((NY,)),
             dma,

time: 44.2 us -> 43.4 us (0.982)
  Pallas kernels: 42.6 us -> 42 us
    pallas_call x1, Pallas kernels: 42.6 us -> 42 us  [local(): pl.pallas_call(kernel, out_shape=pltpu.VMEM((8, columns), f32), in_specs=...]
where the time goes in v5:
time: 43.4 us; the launch traced here: 43.3 us
  Pallas kernels  42 us (97%)
  between operations  0.66 us (2%)
  local copies, waits for them, and re-layouts  0.6 us (1%)
    pallas_call x1, Pallas kernels, local(): pl.pallas_call(kernel, out_shape=pltpu.VMEM((8, columns), f32), in_specs=...  42 us

profile of v5, /device:TPU:1, one launch (start us, length us, event | category | flops | bytes accessed | tf_op | source)
XLA Modules:
  0.0 43.3 jit_solution(16121151207039282964)
XLA Ops:
  0.7 42.0 %attention_step.1 = f32[8,256]{1,0:T(8,128)S(1)} custom-call(s32[1]{0:T(128)S(6)} %copy.13.len_ref, bf16[16,128]{1,0:T(8,128)(2,1)} %bitcast.12, bf16[1,128]{1,0:T(2,128)(2,1)} %bitcast.13, bf16[1,128]{1,0:T(2,128)(2,1)} %bitcast.14, bf16[512,128]{1,0:T(8,128)(2,1)} %bitcast.8, bf16[512,128]{1,0:T(8,128)(2,1)} %bitcast.9, bf16[512,128]{1,0:T(8,128)(2,1)} %bitcast.10, ...), custom_call_target="tpu_custom_call" | custom-call | tf_op jit(solution)/shard_map/attention_step/pallas_call | solution.py:402
  42.7 0.6 %copy.12 = f32[8,256]{1,0:T(8,128)} copy(f32[8,256]{1,0:T(8,128)S(1)} %attention_step.1) | data formatting | bytes 16384

commit v6 on v5

--- a/solution.py
+++ b/solution.py
@@ -214,8 +214,9 @@
         top = jnp.max(s, axis=1, keepdims=True)
         p = jnp.exp2((s - top) * scale).astype(jnp.bfloat16)
         acc = jnp.dot(p, values, preferred_element_type=jnp.float32)
-        acc_out[a] = acc[:, :hd].astype(jnp.bfloat16)
-        st_out[a] = jnp.concatenate([line(top * scale), line(acc[:, hd:])], axis=0)
+        mass = acc[:, hd:]
+        acc_out[a] = (acc[:, :hd] / mass).astype(jnp.bfloat16)
+        st_out[a] = line(top * scale + jnp.log2(mass))
 
     def reply(a):
         for b in (4, 3, 5, 2, 6, 1, 7, 0):
@@ -255,7 +256,7 @@
         for a in group:
             reply(a)
 
-    spot = lax.broadcasted_iota(jnp.int32, (2, rows), 1) // heads
+    spot = lax.broadcasted_iota(jnp.int32, (1, rows), 1) // heads
     joined = []
     landed(st_in.at[pl.ds(0, CHIPS - 1)], st_recv)
     pl.when(moved)(lambda: landed(suf_in, suf_recv))
@@ -265,15 +266,15 @@
         for b in range(1, NZ):
             both = jnp.where(spot == b, st_in[a * NZ + b], both)
         joined.append(both)
-    best = functools.reduce(jnp.maximum, [both[:1] for both in joined])
+    best = functools.reduce(jnp.maximum, joined)
     mine = lax.broadcasted_iota(jnp.int32, (heads, rows), 1) % heads == lax.broadcasted_iota(
         jnp.int32, (heads, rows), 0
     )
     row_max = jnp.maximum(
         jnp.max(jnp.where(mine, best, -3e38), axis=1, keepdims=True), suf_max
     )
-    spread = [jnp.where(mine, jnp.exp2(both[:1] - row_max), 0.0) for both in joined]
-    shares = functools.reduce(jnp.add, [f * both[1:] for f, both in zip(spread, joined)])
+    spread = [jnp.where(mine, jnp.exp2(both - row_max), 0.0) for both in joined]
+    shares = functools.reduce(jnp.add, spread)
     suf_factor = jnp.exp2(suf_max - row_max)
     total = jnp.sum(shares, axis=1, keepdims=True) + suf_mass * suf_factor
     spread = jnp.concatenate(spread, axis=1)
@@ -416,9 +417,9 @@
             pltpu.VMEM((1, page_table.shape[0]), jnp.int32),
             pltpu.VMEM((2, depth, columns), bf16),
             pltpu.VMEM((NY, rows, hd), bf16),
-            pltpu.VMEM((NY, 2, rows), f32),
+            pltpu.VMEM((NY, 1, rows), f32),
             pltpu.VMEM((CHIPS * heads, hd), bf16),
-            pltpu.VMEM((CHIPS, 2, rows), f32),
+            pltpu.VMEM((CHIPS, 1, rows), f32),
             pltpu.VMEM((2 * heads, hd), f32),
             pltpu.VMEM((2 * heads, hd), f32),
             pltpu.VMEM((CHIPS * heads, hd), bf16),

time: 43.4 us -> 43.4 us (level)
  no operation moved by 1% of the time
where the time goes in v6:
time: 43.4 us; the launch traced here: 43.2 us
  Pallas kernels  42 us (97%)
  between operations  0.66 us (2%)
  local copies, waits for them, and re-layouts  0.6 us (1%)
    pallas_call x1, Pallas kernels, local(): pl.pallas_call(kernel, out_shape=pltpu.VMEM((8, columns), f32), in_specs=...  42 us

profile of v6, /device:TPU:1, one launch (start us, length us, event | category | flops | bytes accessed | tf_op | source)
XLA Modules:
  0.0 43.2 jit_solution(11129434415384997160)
XLA Ops:
  0.7 42.0 %attention_step.1 = f32[8,256]{1,0:T(8,128)S(1)} custom-call(s32[1]{0:T(128)S(6)} %copy.13.len_ref, bf16[16,128]{1,0:T(8,128)(2,1)} %bitcast.12, bf16[1,128]{1,0:T(2,128)(2,1)} %bitcast.13, bf16[1,128]{1,0:T(2,128)(2,1)} %bitcast.14, bf16[512,128]{1,0:T(8,128)(2,1)} %bitcast.8, bf16[512,128]{1,0:T(8,128)(2,1)} %bitcast.9, bf16[512,128]{1,0:T(8,128)(2,1)} %bitcast.10, ...), custom_call_target="tpu_custom_call" | custom-call | tf_op jit(solution)/shard_map/attention_step/pallas_call | solution.py:403
  42.6 0.6 %copy.12 = f32[8,256]{1,0:T(8,128)} copy(f32[8,256]{1,0:T(8,128)S(1)} %attention_step.1) | data formatting | bytes 16384
